TPU v7x, 32 devices: a whole 2x2x4 slice. The times are simulated.
32 devices in a mesh: shard: 4 (over z), tensor: 4 (over y, x), section: 2 (over core).
Axes of the slice: x: 2, y: 2, z: 4, core: 2. Of those that a mesh axis runs over, the one named last changes fastest.
Arguments:
- grad_parts: bfloat16 [8, 32, 1024, 1024], P(('tensor', 'section'), None, 'shard')
- weights: bfloat16 [32, 1024, 1024], P(None, 'shard', ('tensor', 'section')), may hold values from -6 to 6
- adam_m: float32 [32, 1024, 1024], P(None, 'shard', ('tensor', 'section'))
- adam_v: float32 [32, 1024, 1024], P(None, 'shard', ('tensor', 'section')), may hold values from 0.01 to 1
- left_stat: float32 [96, 1024, 1024], P('shard', None, ('tensor', 'section')), may hold values from -18 to 18
- right_stat: float32 [96, 1024, 1024], P('shard', None, ('tensor', 'section')), may hold values from -18 to 18
- left_root: bfloat16 [32, 1024, 1024], P(None, 'shard', ('tensor', 'section')), as said below
- right_root: bfloat16 [32, 1024, 1024], P(None, 'shard', ('tensor', 'section')), as said below
- block_owner: int32 [32], replicated, may hold values from 0 to 3, as said below
- block_matrix: int32 [32], replicated, may hold values from 0 to 4, as said below
- factors: float32 [832, 2048], P('shard', ('tensor', 'section')), may hold values from -6 to 6
- factor_grad: bfloat16 [832, 2048], P('shard', ('tensor', 'section')), may hold values from -6 to 6
- factor_m: float32 [832, 2048], P('shard', ('tensor', 'section')), may hold values from -3 to 3
- factor_v: float32 [832, 2048], P('shard', ('tensor', 'section')), may hold values from 0.2 to 2
Outputs:
- new_weights: bfloat16 [32, 1024, 1024], P(None, 'shard')
- adam_m_new: float32 [32, 1024, 1024], P(None, 'shard', ('tensor', 'section'))
- adam_v_new: float32 [32, 1024, 1024], P(None, 'shard', ('tensor', 'section'))
- left_new: float32 [96, 1024, 1024], P('shard', None, ('tensor', 'section'))
- right_new: float32 [96, 1024, 1024], P('shard', None, ('tensor', 'section'))
- factors_new: float32 [832, 2048], P('shard', ('tensor', 'section'))
- factor_m_new: float32 [832, 2048], P('shard', ('tensor', 'section'))
- factor_v_new: float32 [832, 2048], P('shard', ('tensor', 'section'))
Inputs may be any that keep to these rules, and one draw needn't show every extreme that they name: `block_owner`: no owner holds more than 24 blocks, and some owner holds exactly 24. `block_matrix`: matrices 0 to 3 hold 4 blocks each, all other blocks belong to matrix 4. `left_root`: every block is symmetric. `right_root`: every block is symmetric.
All inputs are finite; a program needn't handle non-finite values.
Results may differ from a plain program's by a relative error of at most 0.014.
Values may be sent and summed in bfloat16 or wider, within the bound.
No kernel may reach another device: no remote copies, remote signals or barrier semaphores. Data moves between devices by JAX's collectives and lax.ppermute only.
A program may use at most 384 MiB of HBM per device.

v0:
```python
import jax
import jax.numpy as jnp
from jax import lax
from jax.sharding import PartitionSpec as P

B = 1024
MATS = 5


BETA_ONE = 0.9
BETA_TWO = 0.95
BETA_STAT = 0.95
LEARNING = 0.1
DECAY_RATE = 0.1
EPSILON = 1e-08
FLOOR_RATE = 1e-06
CORRECT_ONE = 1.0 - 0.9**10
CORRECT_TWO = 1.0 - 0.95**10


def adam_direction(grad_float, moment, second):
    moment_new = BETA_ONE * moment + (1.0 - BETA_ONE) * grad_float
    second_new = BETA_TWO * second + (1.0 - BETA_TWO) * grad_float * grad_float
    direction = moment_new / CORRECT_ONE / (jnp.sqrt(second_new / CORRECT_TWO) + EPSILON)
    return (moment_new, second_new, direction)


def slot_numbers(block_owner, capacity):
    positions = jnp.arange(block_owner.shape[0], dtype=jnp.int32)
    earlier = (block_owner[:, None] == block_owner[None, :]) & (
        positions[None, :] < positions[:, None]
    )
    return block_owner * capacity + jnp.sum(earlier.astype(jnp.int32), axis=1)


def slot_contents(slot, slot_total):
    positions = jnp.arange(slot.shape[0], dtype=jnp.int32)
    matches = jnp.arange(slot_total, dtype=jnp.int32)[:, None] == slot[None, :]
    occupied = jnp.any(matches, axis=1)
    block_ids = jnp.sum(jnp.where(matches, positions[None, :], 0), axis=1)
    return (block_ids, occupied)


def fill_slots(tiles, block_ids, occupied):
    picked = jnp.take(tiles, block_ids, axis=0)
    return jnp.where(occupied[:, None, None], picked, jnp.zeros_like(picked))


def shards(
    grad_parts,
    weights,
    adam_m,
    adam_v,
    left_stat,
    right_stat,
    left_root,
    right_root,
    block_owner,
    block_matrix,
    factors,
    factor_grad,
    factor_m,
    factor_v,
):
    capacity = left_stat.shape[0]
    owners = lax.axis_size("shard")
    owner_index = lax.axis_index("shard")
    group_index = lax.axis_index(("tensor", "section"))
    partials = grad_parts[0].astype(jnp.float32)
    gradient = lax.psum_scatter(
        partials.astype(jnp.bfloat16), ("tensor", "section"), scatter_dimension=2, tiled=True
    )
    gradient = lax.optimization_barrier(gradient)
    grad_float = gradient.astype(jnp.float32)
    adam_m_new, adam_v_new, direction = adam_direction(grad_float, adam_m, adam_v)
    matrix_range = jnp.arange(MATS, dtype=jnp.int32)
    onehot = (block_matrix[:, None] == matrix_range[None, :]).astype(jnp.float32)
    adam_part = jnp.sum(jnp.sum(direction * direction, axis=(1, 2))[:, None] * onehot, axis=0)
    slot = slot_numbers(block_owner, capacity)
    block_ids, occupied = slot_contents(slot, owners * capacity)
    slab_width = gradient.shape[2]
    grad_rows, right_rows = (
        lax.all_gather(gradient, ("tensor", "section"), axis=2, tiled=True),
        lax.all_gather(right_root, ("tensor", "section"), axis=2, tiled=True),
    )
    grad_full, right_full, left_cols = (
        lax.all_to_all(
            fill_slots(grad_rows, block_ids, occupied),
            "shard",
            split_axis=0,
            concat_axis=1,
            tiled=True,
        ),
        lax.all_to_all(
            fill_slots(right_rows, block_ids, occupied),
            "shard",
            split_axis=0,
            concat_axis=1,
            tiled=True,
        ),
        lax.all_to_all(
            fill_slots(left_root, block_ids, occupied),
            "shard",
            split_axis=0,
            concat_axis=1,
            tiled=True,
        ),
    )
    first_row = group_index * slab_width
    grad_rows_own = lax.dynamic_slice_in_dim(grad_full, first_row, slab_width, 1)
    grad_cols_own = lax.dynamic_slice_in_dim(grad_full, first_row, slab_width, 2)
    gram_left = jnp.einsum(
        "sik,sjk->sij", grad_full, grad_rows_own, preferred_element_type=jnp.float32
    )
    gram_right = jnp.einsum(
        "ski,skj->sij", grad_full, grad_cols_own, preferred_element_type=jnp.float32
    )
    left_new = BETA_STAT * left_stat + (1.0 - BETA_STAT) * gram_left
    right_new = BETA_STAT * right_stat + (1.0 - BETA_STAT) * gram_right
    mixed = jnp.einsum(
        "sjc,sjk->sck", left_cols, grad_full, preferred_element_type=jnp.float32
    ).astype(jnp.bfloat16)
    precond = jnp.einsum("sck,skj->scj", mixed, right_full, preferred_element_type=jnp.float32)
    own_blocks = lax.dynamic_slice_in_dim(block_ids, owner_index * capacity, capacity)
    own_occupied = lax.dynamic_slice_in_dim(occupied, owner_index * capacity, capacity)
    own_matrix = jnp.take(block_matrix, own_blocks)
    slot_onehot = ((own_matrix[:, None] == matrix_range[None, :]) & own_occupied[:, None]).astype(
        jnp.float32
    )
    shampoo_part = jnp.sum(jnp.sum(precond * precond, axis=(1, 2))[:, None] * slot_onehot, axis=0)
    adam_norm, shampoo_norm = lax.psum((adam_part, shampoo_part), ("shard", "tensor", "section"))
    precond_half = precond.astype(jnp.bfloat16)
    returned = lax.all_to_all(
        lax.all_to_all(
            precond_half, ("tensor", "section"), split_axis=2, concat_axis=1, tiled=True
        ),
        "shard",
        split_axis=1,
        concat_axis=0,
        tiled=True,
    )
    precond_tile = jnp.take(returned, slot, axis=0).astype(jnp.float32)
    counts = jnp.sum(onehot, axis=0) * float(B * B)
    graft_scale = jnp.sqrt(adam_norm / (shampoo_norm + FLOOR_RATE * counts))
    block_scale = jnp.sum(onehot * graft_scale[None, :], axis=1)
    weights_float = weights.astype(jnp.float32)
    updated = (
        weights_float
        - LEARNING * (block_scale[:, None, None] * precond_tile + DECAY_RATE * weights_float)
    ).astype(jnp.bfloat16)
    factor_m_new, factor_v_new, factor_step = adam_direction(
        factor_grad.astype(jnp.float32), factor_m, factor_v
    )
    factors_new = factors - LEARNING * (factor_step + DECAY_RATE * factors)
    new_weights = lax.all_gather(updated, ("tensor", "section"), axis=2, tiled=True)
    return (
        new_weights,
        adam_m_new,
        adam_v_new,
        left_new,
        right_new,
        factors_new,
        factor_m_new,
        factor_v_new,
    )


def solution(mesh):
    in_specs = (
        P(("tensor", "section"), None, "shard", None),
        P(None, "shard", ("tensor", "section")),
        P(None, "shard", ("tensor", "section")),
        P(None, "shard", ("tensor", "section")),
        P("shard", None, ("tensor", "section")),
        P("shard", None, ("tensor", "section")),
        P(None, "shard", ("tensor", "section")),
        P(None, "shard", ("tensor", "section")),
        P(),
        P(),
        P("shard", ("tensor", "section")),
        P("shard", ("tensor", "section")),
        P("shard", ("tensor", "section")),
        P("shard", ("tensor", "section")),
    )
    out_specs = (
        P(None, "shard", None),
        P(None, "shard", ("tensor", "section")),
        P(None, "shard", ("tensor", "section")),
        P("shard", None, ("tensor", "section")),
        P("shard", None, ("tensor", "section")),
        P("shard", ("tensor", "section")),
        P("shard", ("tensor", "section")),
        P("shard", ("tensor", "section")),
    )
    return jax.shard_map(shards, mesh=mesh, in_specs=in_specs, out_specs=out_specs, check_vma=False)
```

profile of v0, /device:TPU:0, one launch (start us, length us, event | category | flops | bytes accessed | tf_op | source)
XLA Modules:
  0.0 3112.9 jit_solution(10936818432663328828)
XLA Ops:
  7.2 0.0 copy-start
  7.2 0.0 reduce-scatter.4.cloned.1.call-start
  7.2 23.8 copy.71
  31.1 17.8 copy.73
  48.9 0.0 reduce-scatter.4.cloned.1.call-update
  48.9 0.0 copy-start.10
  48.9 0.0 all-gather.6.cloned.1.call-start
  49.0 0.7 all-gather.6.cloned.1.call-update
  49.7 0.0 all-gather.4.cloned.1.call-start
  49.7 118.0 %reduce-scatter.4.cloned.1.call-done = bf16[128,8192]{1,0:T(8,128)(2,1)} async-done(((bf16[1024,8192]{1,0:T(8,128)(2,1)}), bf16[128,8192]{1,0:T(8,128)(2,1)}) %reduce-scatter.4.cloned.1.call-update) | async-done | bytes 2097168
  167.7 3.5 copy.74
  171.2 4.5 copy.72
  175.8 0.0 all-gather.4.cloned.1.call-update
  175.8 0.0 copy-done.10
  175.8 0.2 convert_reduce_fusion
  176.0 0.5 compare_and_fusion
  176.5 0.1 select_reduce_fusion
  176.6 6.0 gather_fusion.1
  182.7 0.0 copy-done.11
  182.7 0.1 fusion.19
  182.8 7.0 select_select_fusion.2
  189.8 5.2 all-to-all-start
  195.1 67.7 %all-gather.6.cloned.1.call-done = bf16[32,256,1024]{2,1,0:T(8,128)(2,1)} async-done(((bf16[32,256,128]{2,1,0:T(8,128)(2,1)}), bf16[32,256,1024]{2,1,0:T(8,128)(2,1)}) %all-gather.6.cloned.1.call-update) | async-done | bytes 16777232 | tf_op jit(solution)/shard_map/all_gather | solution.py:84
  262.8 24.7 gather_fusion.4
  287.5 70.9 %all-gather.4.cloned.1.call-done = bf16[32,256,1024]{2,1,0:T(8,128)(2,1)} async-done(((bf16[32,256,128]{2,1,0:T(8,128)(2,1)}), bf16[32,256,1024]{2,1,0:T(8,128)(2,1)}) %all-gather.4.cloned.1.call-update) | async-done | bytes 16777232 | tf_op jit(solution)/shard_map/all_gather | solution.py:83
  358.4 23.2 gather_fusion.3
  381.5 64.7 %select_select_fusion.1 = (bf16[96,256,1024]{2,1,0:T(8,128)(2,1)}, bf16[96,256,1024]{2,1,0:T(8,128)(2,1)}) fusion(bf16[96,256,1024]{2,1,0:T(8,128)(2,1)} %gather_fusion.3, pred[96]{0:T(512)(128)(4,1)S(1)} %compare_and_fusion.1, pred[96]{0:T(512)(128)(4,1)S(1)} %fusion.19, bf16[96,256,1024]{2,1,0:T(8,128)(2,1)} %gather_fusion.4), kind=kLoop, calls=%fused_computation.6 | loop fusion | flops 100663296 | bytes 201326784 | tf_op jit(solution)/shard_map/jit(_where)/select_n | solution.py:46
  446.2 0.0 all-to-all-done
  446.2 1107.8 %all_to_all.90 = bf16[96,256,1024]{2,1,0:T(8,128)(2,1)} all-to-all(bf16[96,256,1024]{2,1,0:T(8,128)(2,1)} %get-tuple-element.23), channel_id=1, replica_groups=mesh['shard'=4,'tensor'=4,'section'=2] {'shard'}, dimensions={0} | all-to-all | bytes 100663296 | tf_op jit(solution)/shard_map/all_to_all | solution.py:87
  1554.0 11.9 all-to-all-start.2
  1566.0 6.3 copy.55
  1572.3 33.4 %copy.56 = bf16[4,24,256,1024]{3,2,0,1:T(8,128)(2,1)} copy(bf16[4,24,256,1024]{3,2,1,0:T(8,128)(2,1)} %bitcast.49) | data formatting | bytes 100663296 | tf_op jit(solution)/shard_map/all_to_all | solution.py:87
  1605.7 1041.9 %all-to-all-done.2 = bf16[96,256,1024]{2,1,0:T(8,128)(2,1)} async-done(((bf16[96,256,1024]{2,1,0:T(8,128)(2,1)}), bf16[96,256,1024]{2,1,0:T(8,128)(2,1)}, u32[]{:S(2)}, u32[]{:S(2)}) %all-to-all-start.2) | async-done | bytes 50331680 | tf_op jit(solution)/shard_map/all_to_all | solution.py:94
  2647.5 33.4 %copy.58 = bf16[4,24,256,1024]{3,2,0,1:T(8,128)(2,1)} copy(bf16[4,24,256,1024]{3,2,1,0:T(8,128)(2,1)} %bitcast.9) | data formatting | bytes 100663296 | tf_op jit(solution)/shard_map/all_to_all | solution.py:94
  2680.9 22.2 fusion.5.clone.4
  2703.2 22.1 multiply_reduce_fusion
  2725.2 8.9 copy.59
  2734.2 76.9 %all_to_all.91 = bf16[24,128,1024]{1,0,2:T(8,128)(2,1)} all-to-all(bf16[24,128,1024]{1,0,2:T(8,128)(2,1)} %copy.59), channel_id=1, replica_groups=mesh['shard'=4,'tensor'=4,'section'=2] {'tensor','section'}, dimensions={2} | all-to-all | bytes 12582912 | tf_op jit(solution)/shard_map/all_to_all | solution.py:134
  2811.1 9.5 copy.69
  2820.6 5.4 all-to-all-start.4
  2826.0 0.0 all-gather.8.cloned.1.call-start
  2826.0 0.0 copy-done.9
  2826.1 0.1 dynamic_slice.13
  2826.1 0.0 copy-done.14
  2826.1 0.1 compare_select_fusion.3
  2826.2 0.7 gather_fusion
  2827.0 0.1 and_select_fusion
  2827.0 9.5 multiply_reduce_fusion.1
  2836.6 0.1 convert_reduce_fusion.1
  2836.7 0.1 select_reduce_fusion.2
  2836.8 146.2 %all-reduce = (f32[5]{0:T(128)S(1)}, f32[5]{0:T(128)S(1)}) all-reduce(f32[5]{0:T(128)S(1)} %get-tuple-element.10, f32[5]{0:T(128)S(1)} %select_reduce_fusion.2), channel_id=1, replica_groups=mesh['shard'=4,'tensor'=4,'section'=2] {'shard','tensor','section'}, use_global_device_ids=true, to_apply=%region_3.0 | all-reduce | flops 10 | bytes 80 | tf_op jit(solution)/shard_map/psum | solution.py:131
  2983.1 0.1 select_reduce_fusion.1
  2983.1 0.0 all-to-all-done.4
  2983.2 0.0 copy-start.7
  2983.2 7.1 copy.64
  2990.3 3.8 gather_fusion.2
  2994.1 4.3 fusion.12
  2998.5 0.0 all-gather.8.cloned.1.call-update
  2998.6 0.9 multiply_subtract_fusion
  2999.5 30.3 multiply_add_fusion
  3029.8 30.2 multiply_add_fusion.1
  3060.0 32.3 %all-gather.8.cloned.1.call-done = bf16[32,256,1024]{2,1,0:T(8,128)(2,1)} async-done(((bf16[32,256,128]{2,1,0:T(8,128)(2,1)}), bf16[32,256,1024]{2,1,0:T(8,128)(2,1)}) %all-gather.8.cloned.1.call-update) | async-done | bytes 16777232 | tf_op jit(solution)/shard_map/all_gather | solution.py:155
  3092.3 14.1 copy.76
  3106.4 0.0 copy-done.1
  (31 shorter events, 0.1 us)
Async XLA Ops:
  7.2 169.5 %copy-start = (bf16[32,256,128]{2,1,0:T(8,128)(2,1)S(1)}, bf16[32,256,128]{2,1,0:T(8,128)(2,1)}, u32[]{:S(2)}) copy-start(bf16[32,256,128]{2,1,0:T(8,128)(2,1)} %param.22) | copy-start | bytes 6291460
  7.2 160.6 %reduce-scatter.4.cloned.1.call-start = ((), (), s32[]{:S(2)}) async-start(), calls=%async_computation.9 | async-start | bytes 18874368
  48.9 126.9 %copy-start.10 = (s32[32]{0:T(128)S(1)}, s32[32]{0:T(128)}, u32[]{:S(2)}) copy-start(s32[32]{0:T(128)} %param.24) | copy-start | bytes 388
  48.9 213.8 %all-gather.6.cloned.1.call-start = ((), (), s32[]{:S(2)}) async-start(), calls=%async_computation.7 | async-start | bytes 18874368 | tf_op jit(solution)/shard_map/all_gather | solution.py:84
  49.7 308.7 %all-gather.4.cloned.1.call-start = ((), (), s32[]{:S(2)}) async-start(), calls=%async_computation.6 | async-start | bytes 18874368 | tf_op jit(solution)/shard_map/all_gather | solution.py:83
  176.5 6.2 copy-start.11
  176.6 18.4 copy-start.13
  182.7 198.8 %copy-start.8 = (pred[96]{0:T(512)(128)(4,1)}, pred[96]{0:T(512)(128)(4,1)S(1)}, u32[]{:S(2)}) copy-start(pred[96]{0:T(512)(128)(4,1)S(1)} %fusion.19) | copy-start | bytes 292
  189.8 256.4 %all-to-all-start = ((bf16[96,256,128]{2,1,0:T(8,128)(2,1)}), bf16[96,256,128]{2,1,0:T(8,128)(2,1)}, u32[]{:S(2)}, u32[]{:S(2)}) async-start(bf16[96,256,128]{2,1,0:T(8,128)(2,1)} %select_select_fusion.2), calls=%async_computation | async-start | bytes 12582912 | tf_op jit(solution)/shard_map/all_to_all | solution.py:101
  1554.0 1093.5 %all-to-all-start.2 = ((bf16[96,256,1024]{2,1,0:T(8,128)(2,1)}), bf16[96,256,1024]{2,1,0:T(8,128)(2,1)}, u32[]{:S(2)}, u32[]{:S(2)}) async-start(bf16[96,256,1024]{2,1,0:T(8,128)(2,1)} %get-tuple-element.24), calls=%async_computation.2 | async-start | bytes 100663296 | tf_op jit(solution)/shard_map/all_to_all | solution.py:94
  2820.6 5.5 copy-start.9
  2820.6 5.5 copy-start.14
  2820.6 5.6 copy-start.2
  2820.6 6.3 copy-start.12
  2820.6 162.5 %all-to-all-start.4 = ((bf16[24,1024,128]{2,0,1:T(8,128)(2,1)}), bf16[24,1024,128]{2,0,1:T(8,128)(2,1)}, u32[]{:S(2)}, u32[]{:S(2)}) async-start(bf16[24,1024,128]{2,0,1:T(8,128)(2,1)} %bitcast.54), calls=%async_computation.4 | async-start | bytes 12582912 | tf_op jit(solution)/shard_map/all_to_all | solution.py:133
  2826.0 266.3 %all-gather.8.cloned.1.call-start = ((), (), s32[]{:S(2)}) async-start(), calls=%async_computation.8 | async-start | bytes 18874368 | tf_op jit(solution)/shard_map/all_gather | solution.py:155
  2983.2 11.0 copy-start.7
  2990.3 8.2 copy-start.3
  2990.3 8.2 copy-start.4
  2990.3 8.2 copy-start.5
  2990.3 8.2 copy-start.6
  3092.3 14.1 copy-start.1
Sparse Core Ops, SparseCore 0:
  49.1 118.6 reduce-scatter.3
  169.6 93.0 all-gather.5
  265.2 93.1 all-gather.3
  2998.6 93.6 all-gather.7
where the time goes:
time: 3120 us; the launch traced here: 3110 us
  waiting for transfers between devices  1330 us (43%)
  blocking collectives  1330 us (43%)
  local copies, waits for them, and re-layouts  221 us (7%)
  matrix products  105 us (3%)
  other arithmetic  87.9 us (3%)
    all_to_all x1, blocking collectives, shards(): lax.all_to_all(fill_slots(grad_rows, block_ids, occupied), 'shard', split...  1110 us
    all_to_all x1, waiting for transfers between devices, shards(): lax.all_to_all(fill_slots(right_rows, block_ids, occupied), 'shard', spli...  1040 us
    psum x1, blocking collectives, shards(): lax.psum((adam_part, shampoo_part), ('shard', 'tensor', 'section'))  146 us
    unnamed x5, waiting for transfers between devices  119 us
    all_to_all x1, blocking collectives, shards(): lax.all_to_all(precond_half, ('tensor', 'section'), split_axis=2, concat_...  76.9 us
    select_n x2, other arithmetic, fill_slots(): return jnp.where(occupied[:, None, None], picked, jnp.zeros_like(picked))  71.7 us
    all_gather x1, waiting for transfers between devices, shards(): lax.all_gather(gradient, ('tensor', 'section'), axis=2, tiled=True)  70.9 us
    all_gather x1, waiting for transfers between devices, shards(): lax.all_gather(right_root, ('tensor', 'section'), axis=2, tiled=True)  67.7 us
  transfers between devices with their start and end apart: 7, of which 5 were waited for; matrix products, arithmetic and copies ran while one was open for 8% of the time, Pallas kernels for 0%

commit v1 on v0

v1 whole, which is shorter than its diff:
```python
import functools

import jax
import jax.numpy as jnp
from jax import lax
from jax.experimental import pallas as pl
from jax.experimental.pallas import tpu as pltpu
from jax.sharding import PartitionSpec as P

MATS = 5

BETA_ONE = 0.9
BETA_TWO = 0.95
BETA_STAT = 0.95
LEARNING = 0.1
DECAY_RATE = 0.1
EPSILON = 1e-08
FLOOR_RATE = 1e-06
CORRECT_ONE = 1.0 - 0.9**10
CORRECT_TWO = 1.0 - 0.95**10

GROUP = ("tensor", "section")
ALL = ("shard", "tensor", "section")
VMEM_LIMIT = 48 * 1024 * 1024
LANES = 128


def params():
    return pltpu.CompilerParams(vmem_limit_bytes=VMEM_LIMIT)


def adam_direction(grad_float, moment, second):
    moment_new = BETA_ONE * moment + (1.0 - BETA_ONE) * grad_float
    second_new = BETA_TWO * second + (1.0 - BETA_TWO) * grad_float * grad_float
    direction = moment_new / CORRECT_ONE / (jnp.sqrt(second_new / CORRECT_TWO) + EPSILON)
    return (moment_new, second_new, direction)


def reorder_kernel(order, block, out):
    out[...] = block[...]


def reorder(blocks, order):
    count = order.shape[0]
    tile = blocks.shape[1:]
    spec = (1,) + tile
    return pl.pallas_call(
        reorder_kernel,
        grid_spec=pltpu.PrefetchScalarGridSpec(
            num_scalar_prefetch=1,
            grid=(count,),
            in_specs=[pl.BlockSpec(spec, lambda i, order: (order[i], 0, 0))],
            out_specs=pl.BlockSpec(spec, lambda i, order: (i, 0, 0)),
        ),
        out_shape=jax.ShapeDtypeStruct((count,) + tile, blocks.dtype),
        compiler_params=params(),
        cost_estimate=pl.CostEstimate(
            flops=0, bytes_accessed=2 * blocks.size * blocks.dtype.itemsize, transcendentals=0
        ),
    )(order, blocks)


def adam_kernel(place, grad, moment, second, moment_out, second_out, total):
    moment_new, second_new, direction = adam_direction(
        grad[0].astype(jnp.float32), moment[0], second[0]
    )
    moment_out[0] = moment_new
    second_out[0] = second_new
    total[0] = jnp.sum(direction * direction, axis=0, keepdims=True)


def adam(grad_tiles, place, moment, second):
    count, rows, cols = moment.shape
    own = pl.BlockSpec((1, rows, cols), lambda i, place: (i, 0, 0))
    return pl.pallas_call(
        adam_kernel,
        grid_spec=pltpu.PrefetchScalarGridSpec(
            num_scalar_prefetch=1,
            grid=(count,),
            in_specs=[
                pl.BlockSpec((1, rows, cols), lambda i, place: (place[i], 0, 0)),
                own,
                own,
            ],
            out_specs=[own, own, pl.BlockSpec((1, 1, cols), lambda i, place: (i, 0, 0))],
        ),
        out_shape=[
            jax.ShapeDtypeStruct(moment.shape, jnp.float32),
            jax.ShapeDtypeStruct(moment.shape, jnp.float32),
            jax.ShapeDtypeStruct((count, 1, cols), jnp.float32),
        ],
        compiler_params=params(),
        cost_estimate=pl.CostEstimate(
            flops=20 * moment.size, bytes_accessed=18 * moment.size, transcendentals=moment.size
        ),
    )(place, grad_tiles, moment, second)


def gram_kernel(chosen, grad, out):
    parts, _, rows, width = grad.shape
    size = parts * rows
    whole = grad[:, 0].reshape(size, width)
    turned = whole.T
    step = 2 * LANES
    for start in range(0, size, step):
        left = lax.dot_general(
            whole,
            whole[start : start + step, :],
            (((1,), (1,)), ((), ())),
            preferred_element_type=jnp.float32,
        ).astype(jnp.bfloat16)
        right = lax.dot_general(
            turned,
            whole[:, start : start + step],
            (((1,), (0,)), ((), ())),
            preferred_element_type=jnp.float32,
        ).astype(jnp.bfloat16)
        for half in range(2):
            slab = start // LANES + half
            out[slab, 0, 0] = left[:, half * LANES : (half + 1) * LANES]
            out[slab, 0, 1] = right[:, half * LANES : (half + 1) * LANES]


def grams(grad_blocks, chosen):
    shards, per, rows, width = grad_blocks.shape
    size = shards * rows
    slabs = size // LANES
    count = chosen.shape[0]
    return pl.pallas_call(
        gram_kernel,
        grid_spec=pltpu.PrefetchScalarGridSpec(
            num_scalar_prefetch=1,
            grid=(count,),
            in_specs=[
                pl.BlockSpec((shards, 1, rows, width), lambda j, chosen: (0, chosen[j], 0, 0))
            ],
            out_specs=pl.BlockSpec(
                (slabs, 1, 2, size, LANES), lambda j, chosen: (0, j, 0, 0, 0)
            ),
        ),
        out_shape=jax.ShapeDtypeStruct((slabs, count, 2, size, LANES), jnp.bfloat16),
        compiler_params=params(),
        cost_estimate=pl.CostEstimate(
            flops=count * 4 * size**3, bytes_accessed=count * 6 * size * size, transcendentals=0
        ),
    )(chosen, grad_blocks)


def stat_kernel(
    source, entry, filled, left_stat, right_stat, left_gram, right_gram, left_out, right_out
):
    full = filled[pl.program_id(0)] > 0
    left = left_gram[0, 0, 0].astype(jnp.float32)
    right = right_gram[0, 0, 0].astype(jnp.float32)
    left_out[0] = BETA_STAT * left_stat[0] + jnp.where(full, (1.0 - BETA_STAT) * left, 0.0)
    right_out[0] = BETA_STAT * right_stat[0] + jnp.where(full, (1.0 - BETA_STAT) * right, 0.0)


def refresh(left_stat, right_stat, received, source, entry, filled):
    slots, size, cols = left_stat.shape
    own = pl.BlockSpec((1, size, cols), lambda r, source, entry, filled: (r, 0, 0))
    gram = (1, 1, 1, size, cols)
    return pl.pallas_call(
        stat_kernel,
        grid_spec=pltpu.PrefetchScalarGridSpec(
            num_scalar_prefetch=3,
            grid=(slots,),
            in_specs=[
                own,
                own,
                pl.BlockSpec(
                    gram, lambda r, source, entry, filled: (source[r], entry[r], 0, 0, 0)
                ),
                pl.BlockSpec(
                    gram, lambda r, source, entry, filled: (source[r], entry[r], 1, 0, 0)
                ),
            ],
            out_specs=[own, own],
        ),
        out_shape=[jax.ShapeDtypeStruct(left_stat.shape, jnp.float32)] * 2,
        compiler_params=params(),
        cost_estimate=pl.CostEstimate(
            flops=6 * left_stat.size, bytes_accessed=20 * left_stat.size, transcendentals=0
        ),
    )(source, entry, filled, left_stat, right_stat, received, received)


def precond_kernel(left, grad, right, out, total):
    slabs, _, rows, cols = left.shape
    parts = grad.shape[0]
    width = grad.shape[3]
    left_rows = jnp.concatenate([left[s, 0] for s in range(slabs)], axis=1)
    whole = grad[:, 0].reshape(parts * rows, width)
    mixed = jnp.dot(left_rows, whole, preferred_element_type=jnp.float32).astype(jnp.bfloat16)
    total[...] = jnp.zeros_like(total)
    step = 2
    for start in range(0, slabs, step):
        columns = jnp.concatenate(
            [right[:, s, 0].reshape(parts * rows, cols) for s in range(start, start + step)], axis=1
        )
        piece = jnp.dot(mixed, columns, preferred_element_type=jnp.float32)
        out[0, :, start * cols : (start + step) * cols] = piece.astype(jnp.bfloat16)
        square = jnp.sum(piece * piece, axis=0, keepdims=True)
        total[0] += square[:, :cols] + square[:, cols:]


def precondition(left, grad_blocks, right):
    shards, per, rows, width = grad_blocks.shape
    slabs, _, _, cols = left.shape
    size = shards * rows
    return pl.pallas_call(
        precond_kernel,
        grid=(per,),
        in_specs=[
            pl.BlockSpec((slabs, 1, rows, cols), lambda m: (0, m, 0, 0)),
            pl.BlockSpec((shards, 1, rows, width), lambda m: (0, m, 0, 0)),
            pl.BlockSpec((shards, slabs, 1, rows, cols), lambda m: (0, 0, m, 0, 0)),
        ],
        out_specs=[
            pl.BlockSpec((1, rows, width), lambda m: (m, 0, 0)),
            pl.BlockSpec((1, 1, cols), lambda m: (m, 0, 0)),
        ],
        out_shape=[
            jax.ShapeDtypeStruct((per, rows, width), jnp.bfloat16),
            jax.ShapeDtypeStruct((per, 1, cols), jnp.float32),
        ],
        compiler_params=params(),
        cost_estimate=pl.CostEstimate(
            flops=per * 4 * rows * size * size,
            bytes_accessed=per * (4 * size * size + 4 * rows * size),
            transcendentals=0,
        ),
    )(left, grad_blocks, right)


def update_kernel(scale, weights, precond, out):
    slabs = weights.shape[0]
    factor = scale[pl.program_id(0)]
    old = jnp.concatenate([weights[s, 0] for s in range(slabs)], axis=1).astype(jnp.float32)
    step = factor * precond[0].astype(jnp.float32) + DECAY_RATE * old
    out[0] = (old - LEARNING * step).astype(jnp.bfloat16)


def update(weights, precond, scale):
    slabs, per, rows, cols = weights.shape
    width = slabs * cols
    own = pl.BlockSpec((1, rows, width), lambda m, scale: (m, 0, 0))
    return pl.pallas_call(
        update_kernel,
        grid_spec=pltpu.PrefetchScalarGridSpec(
            num_scalar_prefetch=1,
            grid=(per,),
            in_specs=[
                pl.BlockSpec((slabs, 1, rows, cols), lambda m, scale: (0, m, 0, 0)),
                own,
            ],
            out_specs=own,
        ),
        out_shape=jax.ShapeDtypeStruct((per, rows, width), jnp.bfloat16),
        compiler_params=params(),
        cost_estimate=pl.CostEstimate(
            flops=5 * weights.size, bytes_accessed=6 * weights.size, transcendentals=0
        ),
    )(scale, weights, precond)


def shards(
    grad_parts,
    weights,
    adam_m,
    adam_v,
    left_stat,
    right_stat,
    left_root,
    right_root,
    block_owner,
    block_matrix,
    factors,
    factor_grad,
    factor_m,
    factor_v,
):
    capacity = left_stat.shape[0]
    blocks, rows, cols = weights.shape
    size = left_stat.shape[1]
    group = size // cols
    per = blocks // group
    sends = -(-capacity // group)
    owner_index = lax.axis_index("shard")
    group_index = lax.axis_index(GROUP)

    ids = jnp.arange(blocks, dtype=jnp.int32)
    before = (block_owner[None, :] < block_owner[:, None]) | (
        (block_owner[None, :] == block_owner[:, None]) & (ids[None, :] < ids[:, None])
    )
    position = jnp.sum(before.astype(jnp.int32), axis=1)
    place = (position % group) * per + position // group
    order = jnp.sum(jnp.where(place[None, :] == ids[:, None], ids[None, :], 0), axis=1)

    first = jnp.sum((block_owner < owner_index).astype(jnp.int32))
    held = jnp.sum((block_owner == owner_index).astype(jnp.int32))
    own_entry = (first - group_index + group - 1) // group
    chosen = jnp.minimum(own_entry + jnp.arange(sends, dtype=jnp.int32), per - 1)
    ranks = jnp.arange(capacity, dtype=jnp.int32)
    source = (first + ranks) % group
    entry = (first + ranks) // group - (first - source + group - 1) // group
    filled = (ranks < held).astype(jnp.int32)
    entry = jnp.where(ranks < held, entry, 0)

    def deal(tiles):
        sent = reorder(tiles, order).reshape(group, per, rows, cols)
        return lax.all_to_all(sent, GROUP, split_axis=0, concat_axis=0, tiled=True)

    partials = reorder(grad_parts[0], order)
    gradient = lax.psum_scatter(partials, GROUP, scatter_dimension=0, tiled=True)
    right_dealt = deal(right_root)
    right_blocks = lax.all_gather(right_dealt, "shard", axis=0)
    left_dealt = deal(left_root)
    weights_dealt = deal(weights)
    grad_blocks = lax.all_gather(gradient, "shard", axis=0)

    tiles = jnp.transpose(gradient.reshape(per, rows, group, cols), (2, 0, 1, 3))
    tiles = lax.all_to_all(tiles, GROUP, split_axis=0, concat_axis=0, tiled=True)
    adam_m_new, adam_v_new, adam_total = adam(
        tiles.reshape(blocks, rows, cols), place, adam_m, adam_v
    )

    precond, precond_total = precondition(left_dealt, grad_blocks, right_blocks)

    matrix_range = jnp.arange(MATS, dtype=jnp.int32)
    onehot = (block_matrix[:, None] == matrix_range[None, :]).astype(jnp.float32)
    own_order = lax.dynamic_slice_in_dim(order, group_index * per, per)
    own_onehot = jnp.sum(
        jnp.where((own_order[:, None] == ids[None, :])[:, :, None], onehot[None, :, :], 0.0), axis=1
    )
    adam_part = jnp.sum(jnp.sum(adam_total, axis=(1, 2))[:, None] * onehot, axis=0)
    shampoo_part = jnp.sum(jnp.sum(precond_total, axis=(1, 2))[:, None] * own_onehot, axis=0)
    adam_norm, shampoo_norm = lax.psum((adam_part, shampoo_part), ALL)
    counts = jnp.sum(onehot, axis=0) * float(size * size)
    graft_scale = jnp.sqrt(adam_norm / (shampoo_norm + FLOOR_RATE * counts))
    block_scale = jnp.sum(own_onehot * graft_scale[None, :], axis=1)

    updated = update(weights_dealt, precond, block_scale)
    gathered = lax.all_gather(updated, GROUP, axis=0, tiled=True)
    new_weights = reorder(gathered, place)

    slabs = grams(grad_blocks, chosen)
    received = lax.all_to_all(slabs, GROUP, split_axis=0, concat_axis=0, tiled=True)
    left_new, right_new = refresh(left_stat, right_stat, received, source, entry, filled)

    factor_m_new, factor_v_new, factor_step = adam_direction(
        factor_grad.astype(jnp.float32), factor_m, factor_v
    )
    factors_new = factors - LEARNING * (factor_step + DECAY_RATE * factors)
    return (
        new_weights,
        adam_m_new,
        adam_v_new,
        left_new,
        right_new,
        factors_new,
        factor_m_new,
        factor_v_new,
    )


def solution(mesh):
    tile = P(None, "shard", GROUP)
    stat = P("shard", None, GROUP)
    factor = P("shard", GROUP)
    in_specs = (P(GROUP, None, "shard", None), tile, tile, tile, stat, stat, tile, tile, P(), P())
    out_specs = (P(None, "shard", None), tile, tile, stat, stat)
    return jax.shard_map(
        shards,
        mesh=mesh,
        in_specs=in_specs + (factor,) * 4,
        out_specs=out_specs + (factor,) * 3,
        check_vma=False,
    )
```

time: 3120 us -> 696 us (0.22)
  blocking collectives: 1330 us -> 70.2 us
  waiting for transfers between devices: 1330 us -> 440 us
  local copies, waits for them, and re-layouts: 221 us -> 14.2 us
  Pallas kernels: 0 us -> 130 us
  matrix products: 105 us -> 0 us
  other arithmetic: 87.9 us -> 5.52 us
    all_to_all x2 -> x1, blocking collectives: 1180 us -> 31.7 us  [deal(): return lax.all_to_all(sent, GROUP, split_axis=0, concat_axis=0, tiled=True)]
    all_to_all x3 -> x4, waiting for transfers between devices: 1040 us -> 232 us  [the longest x1 187 us: shards(): lax.all_to_all(slabs, GROUP, split_axis=0, concat_axis=0, tiled=True)]
    pallas_call x0 -> x10, Pallas kernels: none -> 130 us  [the longest x5 49.1 us: reorder(): pl.pallas_call(reorder_kernel, grid_spec=pltpu.PrefetchScalarGridSpec(num...]
    unnamed x5 -> x4, waiting for transfers between devices: 119 us -> 0.07 us
    psum x1, blocking collectives: 146 us -> 38.5 us  [shards(): adam_norm, shampoo_norm = lax.psum((adam_part, shampoo_part), ALL)]
    dot_general x4 -> x0, matrix products: 105 us -> none  [the longest x1 30.3 us: shards(): jnp.einsum('ski,skj->sij', grad_full, grad_cols_own, preferred_element_ty...]
    all_to_all x5 -> x0, local copies, waits for them, and re-layouts: 89.7 us -> none  [the longest x1 33.4 us: shards(): lax.all_to_all(fill_slots(right_rows, block_ids, occupied), 'shard', spli...]
    reduce_scatter x0 -> x1, waiting for transfers between devices: none -> 84.3 us  [shards(): lax.psum_scatter(partials, GROUP, scatter_dimension=0, tiled=True)]
  transfers between devices with their start and end apart: 7 -> 8, of which waited for: 5 -> 5; matrix products, arithmetic and copies ran while one was open for 8% -> 1% of each run, Pallas kernels for 0% -> 11%
where the time goes in v1:
time: 696 us; the launch traced here: 694 us
  waiting for transfers between devices  440 us (63%)
  Pallas kernels  130 us (19%)
  blocking collectives  70.2 us (10%)
  starting transfers between devices  17.4 us (2%)
  between operations  16.4 us (2%)
  local copies, waits for them, and re-layouts  14.2 us (2%)
    all_to_all x1, waiting for transfers between devices, shards(): lax.all_to_all(slabs, GROUP, split_axis=0, concat_axis=0, tiled=True)  187 us
    all_gather x1, waiting for transfers between devices, shards(): grad_blocks = lax.all_gather(gradient, 'shard', axis=0)  123 us
    reduce_scatter x1, waiting for transfers between devices, shards(): lax.psum_scatter(partials, GROUP, scatter_dimension=0, tiled=True)  84.3 us
    pallas_call x5, Pallas kernels, reorder(): pl.pallas_call(reorder_kernel, grid_spec=pltpu.PrefetchScalarGridSpec(num...  49.1 us
    psum x1, blocking collectives, shards(): adam_norm, shampoo_norm = lax.psum((adam_part, shampoo_part), ALL)  38.5 us
    all_to_all x1, blocking collectives, deal(): return lax.all_to_all(sent, GROUP, split_axis=0, concat_axis=0, tiled=True)  31.7 us
    pallas_call x1, Pallas kernels, refresh(): pl.pallas_call(stat_kernel, grid_spec=pltpu.PrefetchScalarGridSpec(num_sc...  28.5 us
    all_to_all x2, waiting for transfers between devices, deal(): return lax.all_to_all(sent, GROUP, split_axis=0, concat_axis=0, tiled=True)  23.1 us
  transfers between devices with their start and end apart: 8, of which 5 were waited for; matrix products, arithmetic and copies ran while one was open for 1% of the time, Pallas kernels for 11%

profile of v1, /device:TPU:0, one launch (start us, length us, event | category | flops | bytes accessed | tf_op | source)
XLA Modules:
  0.0 693.5 jit_solution(15436403091569921713)
XLA Ops:
  8.0 0.0 reduce-scatter.2.cloned.1.call-start
  8.0 0.9 convert_reduce_fusion
  9.0 0.1 select_reduce_fusion.order
  9.1 22.9 %shard_map.197 = bf16[32,256,1024]{2,1,0:T(8,128)(2,1)} custom-call(s32[32]{0:T(128)S(1)} %select_reduce_fusion.order, bf16[32,256,1024]{2,1,0:T(8,128)(2,1)} %bitcast.17), custom_call_target="tpu_custom_call" | custom-call | bytes 33554432 | tf_op jit(solution)/shard_map/pallas_call | solution.py:47
  31.9 0.0 reduce-scatter.2.cloned.1.call-update
  32.0 0.0 all-gather.10.cloned.1.call-start
  32.0 1.5 copy-done.5
  33.5 1.1 shard_map.200
  34.7 31.7 %all_to_all.25 = bf16[8,4,256,128]{3,2,1,0:T(8,128)(2,1)} all-to-all(bf16[8,4,256,128]{3,2,1,0:T(8,128)(2,1)S(1)} %bitcast.16), channel_id=1, replica_groups=mesh['shard'=4,'tensor'=4,'section'=2] {'tensor','section'}, dimensions={0} | all-to-all | bytes 4194304 | tf_op jit(solution)/shard_map/all_to_all | solution.py:312
  66.4 0.0 all-gather.10.cloned.1.call-update
  66.4 0.0 all-gather.8.cloned.1.call-start
  66.4 84.3 %reduce-scatter.2.cloned.1.call-done = bf16[4,256,1024]{2,1,0:T(8,128)(2,1)} async-done(((bf16[32,256,1024]{2,1,0:T(8,128)(2,1)}), bf16[4,256,1024]{2,1,0:T(8,128)(2,1)}) %reduce-scatter.2.cloned.1.call-update) | async-done | bytes 2097168 | tf_op jit(solution)/shard_map/reduce_scatter | solution.py:315
  150.8 0.0 all-gather.8.cloned.1.call-update
  150.8 0.0 copy-done.6
  150.8 1.1 shard_map.199
  152.0 0.0 copy-start.3
  152.0 1.3 copy-done.3
  153.3 3.6 all-to-all-start.1
  156.9 3.5 bitcast_bitcast_fusion
  160.4 23.1 %all-to-all-done.1.left = bf16[8,4,256,128]{3,2,1,0:T(8,128)(2,1)S(1)} async-done(((bf16[8,4,256,128]{3,2,1,0:T(8,128)(2,1)}), bf16[8,4,256,128]{3,2,1,0:T(8,128)(2,1)S(1)}, u32[]{:S(2)}, u32[]{:S(2)}) %all-to-all-start.1) | async-done | bytes 2097184 | tf_op jit(solution)/shard_map/all_to_all | solution.py:312
  183.5 1.3 copy-done
  184.8 4.4 all-to-all-start
  189.2 0.0 copy-start.7
  189.2 1.6 copy-done.7
  190.7 1.1 shard_map.202
  191.9 0.0 copy-start.2
  191.9 1.3 copy-done.2
  193.2 22.6 %all-to-all-done = bf16[8,4,256,128]{3,2,1,0:T(8,128)(2,1)} async-done(((bf16[8,4,256,128]{3,2,1,0:T(8,128)(2,1)}), bf16[8,4,256,128]{3,2,1,0:T(8,128)(2,1)}, u32[]{:S(2)}, u32[]{:S(2)}) %all-to-all-start) | async-done | bytes 2097184 | tf_op jit(solution)/shard_map/all_to_all | solution.py:323
  215.8 3.7 all-to-all-start.3
  219.6 0.0 all-gather.6.cloned.1.call-start
  219.6 0.1 dynamic_slice.3
  219.7 0.1 iota_compare_fusion.3
  219.8 0.0 copy-done.12
  219.8 0.1 select_reduce_fusion.1
  219.9 20.8 %shard_map.198 = (f32[32,256,128]{2,1,0:T(8,128)}, f32[32,256,128]{2,1,0:T(8,128)}, f32[32,1,128]{2,1,0:T(1,128)S(1)}) custom-call(s32[32]{0:T(128)S(1)} %fusion.7.place.order, bf16[32,256,128]{2,1,0:T(8,128)(2,1)} %bitcast.2.grad, f32[32,256,128]{2,1,0:T(8,128)} %moment.1, f32[32,256,128]{2,1,0:T(8,128)} %second.1), custom_call_target="tpu_custom_call" | custom-call | flops 20971520 | bytes 18874368 | tf_op jit(solution)/shard_map/pallas_call | solution.py:75
  240.6 0.3 reduce_sum.102
  240.9 0.1 fusion.5
  241.1 0.0 all-gather.10.cloned.1.call-done
  241.1 123.4 %all-gather.8.cloned.1.call-done = bf16[16,256,1024]{2,1,0:T(8,128)(2,1)} async-done(((bf16[4,256,1024]{2,1,0:T(8,128)(2,1)}), bf16[16,256,1024]{2,1,0:T(8,128)(2,1)}) %all-gather.8.cloned.1.call-update) | async-done | bytes 8388624 | tf_op jit(solution)/shard_map/all_gather | solution.py:320
  364.5 1.6 copy-done.1
  366.1 8.6 %shard_map.201 = (bf16[4,256,1024]{2,1,0:T(8,128)(2,1)S(1)}, f32[4,1,128]{2,1,0:T(1,128)S(1)}) custom-call(bf16[8,4,256,128]{3,2,1,0:T(8,128)(2,1)S(1)} %copy-done.1, bf16[4,4,256,1024]{3,2,1,0:T(8,128)(2,1)} %bitcast.18, bf16[4,8,4,256,128]{4,3,2,1,0:T(8,128)(2,1)} %bitcast.20), custom_call_target="tpu_custom_call" | custom-call | flops 4294967296 | bytes 20971520 | tf_op jit(solution)/shard_map/pallas_call | solution.py:211
  374.7 0.0 copy-start.4
  374.7 1.3 copy-done.4
  376.0 0.1 reduce_sum.104
  376.1 0.1 multiply_reduce_fusion.1
  376.3 38.5 %all-reduce = (f32[5]{0:T(128)S(1)}, f32[5]{0:T(128)S(1)}) all-reduce(f32[5]{0:T(128)S(1)} %get-tuple-element.25, f32[5]{0:T(128)S(1)} %multiply_reduce_fusion.1), channel_id=1, replica_groups=mesh['shard'=4,'tensor'=4,'section'=2] {'shard','tensor','section'}, use_global_device_ids=true, to_apply=%region_6.7 | all-reduce | flops 10 | bytes 80 | tf_op jit(solution)/shard_map/psum | solution.py:338
  414.8 0.1 multiply_reduce_fusion.scale
  414.9 0.0 all-to-all-done.3.weights
  414.9 4.8 shard_map.203
  419.7 0.0 all-gather.6.cloned.1.call-update
  419.8 0.6 copy-done.13
  420.4 0.6 fusion.9
  421.7 17.8 %shard_map.205 = bf16[8,3,2,1024,128]{4,3,2,1,0:T(8,128)(2,1)} custom-call(s32[3]{0:T(128)S(1)} %add_minimum_fusion.chosen, bf16[4,4,256,1024]{3,2,1,0:T(8,128)(2,1)} %bitcast.19), custom_call_target="tpu_custom_call" | custom-call | flops 12884901888 | bytes 18874368 | tf_op jit(solution)/shard_map/pallas_call | solution.py:129
  439.5 5.5 all-to-all-start.4
  445.0 0.7 compare_convert_fusion.2.filled
  445.7 1.3 and_select_fusion.2
  447.0 0.0 copy-done.8
  447.0 0.0 copy-done.9
  447.0 0.0 copy-done.10
  447.1 0.0 copy-done.11
  447.1 0.9 multiply_subtract_fusion
  448.0 186.7 %all-to-all-done.4.left_gram.right_gram = bf16[8,3,2,1024,128]{4,3,2,1,0:T(8,128)(2,1)} async-done(((bf16[8,3,2,1024,128]{4,3,2,1,0:T(8,128)(2,1)}), bf16[8,3,2,1024,128]{4,3,2,1,0:T(8,128)(2,1)}, u32[]{:S(2)}, u32[]{:S(2)}) %all-to-all-start.4) | async-done | bytes 12582944 | tf_op jit(solution)/shard_map/all_to_all | solution.py:348
  634.7 28.5 %shard_map.206 = (f32[24,1024,128]{2,1,0:T(8,128)}, f32[24,1024,128]{2,1,0:T(8,128)}) custom-call(s32[24]{0:T(128)S(1)} %get-tuple-element.31.source, s32[24]{0:T(128)S(1)} %get-tuple-element.32.entry, s32[24]{0:T(128)S(1)} %compare_convert_fusion.2.filled, f32[24,1024,128]{2,1,0:T(8,128)} %left_stat.1, f32[24,1024,128]{2,1,0:T(8,128)} %right_stat.1, ...), custom_call_target="tpu_custom_call" | custom-call | flops 18874368 | bytes 62914560 | tf_op jit(solution)/shard_map/pallas_call | solution.py:163
  663.3 22.8 %shard_map.204 = bf16[32,256,1024]{2,1,0:T(8,128)(2,1)} custom-call(s32[32]{0:T(128)S(1)} %fusion.7.place.order, bf16[32,256,1024]{2,1,0:T(8,128)(2,1)} %all-gather.6.cloned.1.call-done.block), custom_call_target="tpu_custom_call" | custom-call | bytes 33554432 | tf_op jit(solution)/shard_map/pallas_call | solution.py:47
  (15 shorter events, 0.1 us)
Async XLA Ops:
  8.0 142.8 %reduce-scatter.2.cloned.1.call-start = ((), (), s32[]{:S(2)}) async-start(), calls=%async_computation.6 | async-start | bytes 18874368 | tf_op jit(solution)/shard_map/reduce_scatter | solution.py:315
  31.9 1.6 copy-start.5
  32.0 209.2 %all-gather.10.cloned.1.call-start = ((), (), s32[]{:S(2)}) async-start(), calls=%async_computation.9 | async-start | bytes 10485760 | tf_op jit(solution)/shard_map/all_gather | solution.py:317
  66.3 84.5 %copy-start.6 = (bf16[32,256,128]{2,1,0:T(8,128)(2,1)S(1)}, bf16[32,256,128]{2,1,0:T(8,128)(2,1)}, u32[]{:S(2)}) copy-start(bf16[32,256,128]{2,1,0:T(8,128)(2,1)} %block.3) | copy-start | bytes 6291460
  66.4 298.1 %all-gather.8.cloned.1.call-start = ((), (), s32[]{:S(2)}) async-start(), calls=%async_computation.8 | async-start | bytes 10485760 | tf_op jit(solution)/shard_map/all_gather | solution.py:320
  152.0 1.3 copy-start.3
  153.3 30.2 %all-to-all-start.1 = ((bf16[8,4,256,128]{3,2,1,0:T(8,128)(2,1)}), bf16[8,4,256,128]{3,2,1,0:T(8,128)(2,1)S(1)}, u32[]{:S(2)}, u32[]{:S(2)}) async-start(bf16[8,4,256,128]{3,2,1,0:T(8,128)(2,1)} %bitcast.15), calls=%async_computation.2 | async-start | bytes 4194304 | tf_op jit(solution)/shard_map/all_to_all | solution.py:312
  183.5 1.3 copy-start
  184.8 31.0 %all-to-all-start = ((bf16[8,4,256,128]{3,2,1,0:T(8,128)(2,1)}), bf16[8,4,256,128]{3,2,1,0:T(8,128)(2,1)}, u32[]{:S(2)}, u32[]{:S(2)}) async-start(bf16[8,4,256,128]{3,2,1,0:T(8,128)(2,1)} %bitcast_bitcast_fusion), calls=%async_computation.1 | async-start | bytes 4194304 | tf_op jit(solution)/shard_map/all_to_all | solution.py:323
  189.2 1.6 copy-start.7
  191.9 1.3 copy-start.2
  215.8 4.0 copy-start.12
  215.8 199.1 %all-to-all-start.3 = ((bf16[8,4,256,128]{3,2,1,0:T(8,128)(2,1)}), bf16[8,4,256,128]{3,2,1,0:T(8,128)(2,1)S(1)}, u32[]{:S(2)}, u32[]{:S(2)}) async-start(bf16[8,4,256,128]{3,2,1,0:T(8,128)(2,1)} %bitcast.14), calls=%async_computation.4 | async-start | bytes 4194304 | tf_op jit(solution)/shard_map/all_to_all | solution.py:312
  219.6 443.7 %all-gather.6.cloned.1.call-start = ((), (), s32[]{:S(2)}) async-start(), calls=%async_computation.7 | async-start | bytes 18874368 | tf_op jit(solution)/shard_map/all_gather | solution.py:344
  364.5 1.6 copy-start.1
  374.7 1.3 copy-start.4
  419.7 0.7 copy-start.13
  439.5 7.5 %copy-start.8 = (f32[208,256]{1,0:T(8,128)S(1)}, f32[208,256]{1,0:T(8,128)}, u32[]{:S(2)}) copy-start(f32[208,256]{1,0:T(8,128)} %param.24) | copy-start | bytes 638980
  439.5 7.5 %copy-start.9 = (f32[208,256]{1,0:T(8,128)S(1)}, f32[208,256]{1,0:T(8,128)}, u32[]{:S(2)}) copy-start(f32[208,256]{1,0:T(8,128)} %param.26) | copy-start | bytes 638980
  439.5 7.5 %copy-start.10 = (f32[208,256]{1,0:T(8,128)S(1)}, f32[208,256]{1,0:T(8,128)}, u32[]{:S(2)}) copy-start(f32[208,256]{1,0:T(8,128)} %param.27) | copy-start | bytes 638980
  439.5 7.5 %copy-start.11 = (bf16[208,256]{1,0:T(8,128)(2,1)S(1)}, bf16[208,256]{1,0:T(8,128)(2,1)}, u32[]{:S(2)}) copy-start(bf16[208,256]{1,0:T(8,128)(2,1)} %param.25) | copy-start | bytes 319492
  439.5 195.2 %all-to-all-start.4 = ((bf16[8,3,2,1024,128]{4,3,2,1,0:T(8,128)(2,1)}), bf16[8,3,2,1024,128]{4,3,2,1,0:T(8,128)(2,1)}, u32[]{:S(2)}, u32[]{:S(2)}) async-start(bf16[8,3,2,1024,128]{4,3,2,1,0:T(8,128)(2,1)} %shard_map.205), calls=%async_computation.5 | async-start | bytes 25165824 | tf_op jit(solution)/shard_map/all_to_all | solution.py:348
Sparse Core Ops, SparseCore 0:
  32.1 118.6 reduce-scatter.1
  419.9 183.1 all-gather.5
Sparse Core Ops, SparseCore 1:
  66.5 148.8 all-gather.9
  216.8 147.7 all-gather.7
